TPU v7x, 256 devices: a whole 4x4x8 slice. The times are simulated.
256 devices in a mesh: dp: 16 (over z, core), expert: 4 (over y), blk: 4 (over x).
Axes of the slice: x: 4, y: 4, z: 8, core: 2. Of those that a mesh axis runs over, the one named last changes fastest.
Arguments:
- tokens: bfloat16 [2048, 6144], P('dp', 'blk'), may hold values from -6 to 6
- expert_ids: int32 [2048, 2], P('dp'), may hold values from 0 to 7, all different within a row; in each aligned block of 128 rows (0 to 127, 128 to 255, ...) at most 48 rows name the same one
- route_weights: float32 [2048, 2], P('dp'), may hold values from 0.1 to 1
- gate_weight: bfloat16 [8, 6144, 8192], P('expert', 'blk', 'dp'), may hold values from -0.078125 to 0.078125
- up_weight: bfloat16 [8, 6144, 8192], P('expert', 'blk', 'dp'), may hold values from -0.078125 to 0.078125
- down_weight: bfloat16 [8, 8192, 6144], P('expert', 'dp', 'blk'), may hold values from -0.0625 to 0.0625
Outputs:
- mixed: bfloat16 [2048, 6144], P('dp', 'blk')
Inputs may be any that keep to these rules, and one draw needn't show every extreme that they name: `expert_ids`: each row names 2 different experts. Among the 128 rows of one data shard no expert is named more than 48 times, and in every draw some expert is named exactly 48 times in some shard.
All inputs are finite; a program needn't handle non-finite values.
Results may differ from a plain program's by a relative error of at most 0.0051.
Values may be sent and summed in bfloat16 or wider, within the bound.
A program may use at most 64 MiB of HBM per device.

v0:
```python
import jax
import jax.numpy as jnp
from jax import lax
from jax.sharding import PartitionSpec as P

EXPERTS = 8
CAP = 48


def local(tokens, expert_ids, route_weights, gate_weight, up_weight, down_weight):
    local_count = gate_weight.shape[0]
    token_count = tokens.shape[0]
    top_count = expert_ids.shape[1]
    group_index = lax.axis_index("expert")
    flat_ids = expert_ids.reshape(-1)
    one_hot = (flat_ids[:, None] == jnp.arange(EXPERTS, dtype=jnp.int32)[None, :]).astype(jnp.int32)
    before = jnp.cumsum(one_hot, axis=0) - one_hot
    position = jnp.sum(before * one_hot, axis=1)
    local_ids = flat_ids - group_index * local_count
    is_mine = local_ids[:, None] == jnp.arange(local_count, dtype=jnp.int32)[None, :]
    in_slot = position[:, None] == jnp.arange(CAP, dtype=jnp.int32)[None, :]
    slot_hit = (is_mine[:, :, None] & in_slot[:, None, :]).reshape(
        token_count, top_count, local_count, CAP
    )
    dispatch = jnp.any(slot_hit, axis=1).astype(jnp.bfloat16)
    combine = jnp.sum(slot_hit.astype(jnp.float32) * route_weights[:, :, None, None], axis=1)
    picked = jnp.einsum("tec,tf->ecf", dispatch, tokens, preferred_element_type=jnp.float32).astype(
        jnp.bfloat16
    )
    shard_rows = lax.all_gather(picked, "dp", axis=1, tiled=True)
    gate_part = jnp.einsum(
        "enf,efh->enh", shard_rows, gate_weight, preferred_element_type=jnp.float32
    )
    up_part = jnp.einsum("enf,efh->enh", shard_rows, up_weight, preferred_element_type=jnp.float32)
    partial_value = jnp.stack([gate_part, up_part])
    summed = lax.psum(partial_value, "blk")
    hidden = (jax.nn.silu(summed[0]) * summed[1]).astype(jnp.bfloat16)
    expert_out = lax.psum_scatter(
        jnp.einsum("enh,ehd->ned", hidden, down_weight, preferred_element_type=jnp.float32),
        "dp",
        scatter_dimension=0,
        tiled=True,
    )
    mixed_part = jnp.einsum("tec,ced->td", combine, expert_out, precision=lax.Precision.HIGHEST)
    mixed = lax.psum(mixed_part, "expert")
    return mixed.astype(jnp.bfloat16)


def solution(mesh):
    placed = (
        P("dp", "blk"),
        P("dp", None),
        P("dp", None),
        P("expert", "blk", "dp"),
        P("expert", "blk", "dp"),
        P("expert", "dp", "blk"),
    )
    return jax.shard_map(
        local, mesh=mesh, in_specs=placed, out_specs=P("dp", "blk"), check_vma=False
    )
```

profile of v0, /device:TPU:2, one launch (start us, length us, event | category | flops | bytes accessed | tf_op | source)
XLA Modules:
  0.0 316.2 jit_solution(18314517861227424447)
XLA Ops:
  6.5 0.9 copy.13
  7.5 0.1 eq.65
  7.6 0.1 reshape.70
  7.8 0.6 reduce-window.6
  8.4 0.2 slice_reduce_fusion
  8.6 0.1 fusion.7
  8.7 0.1 eq.69
  8.9 0.1 copy.15
  9.0 0.7 broadcast_subtract_fusion
  9.7 1.9 convolution_convert_fusion
  11.7 0.0 all-reduce.3.cloned.1.call-start
  11.7 45.8 %all-gather.2.cloned.1.call-done = bf16[2,768,1536]{2,1,0:T(8,128)(2,1)} async-done(((bf16[2,48,1536]{2,1,0:T(8,128)(2,1)}), bf16[2,768,1536]{2,1,0:T(8,128)(2,1)}) %all-gather.2.cloned.1.call-update) | async-done | bytes 4718608 | tf_op jit(solution)/shard_map/all_gather | solution.py:30
  57.5 5.5 %convolution_bitcast_fusion.2 = f32[1,2,768,512]{3,2,1,0:T(8,128)S(1)} fusion(bf16[2,768,1536]{2,1,0:T(8,128)(2,1)} %all-gather.2.cloned.1.call-done, bf16[2,1536,512]{2,1,0:T(8,128)(2,1)} %param.10), kind=kOutput, calls=%fused_computation.8 | convolution fusion | flops 2415919104 | bytes 11010048 | tf_op jit(solution)/shard_map/enf,efh->enh/dot_general | solution.py:34
  63.0 0.1 copy-done.3
  63.1 2.6 convolution_bitcast_fusion.3
  65.7 3.4 %pad_maximum_fusion = f32[2,2,768,512]{3,2,1,0:T(8,128)} fusion(f32[1,2,768,512]{3,2,1,0:T(8,128)S(1)} %convolution_bitcast_fusion.2, f32[1,2,768,512]{3,2,1,0:T(8,128)S(1)} %convolution_bitcast_fusion.3), kind=kLoop, calls=%fused_computation | loop fusion | flops 1572864 | bytes 12582912 | tf_op jit(solution)/shard_map/stack | solution.py:35
  69.1 0.0 all-reduce.3.cloned.1.call-update
  69.1 0.0 reduce-scatter.2.cloned.1.call-start
  69.1 129.7 %all-reduce.3.cloned.1.call-done = f32[2,2,768,512]{3,2,1,0:T(8,128)} async-done(((f32[2,2,768,512]{3,2,1,0:T(8,128)}), f32[2,2,768,512]{3,2,1,0:T(8,128)}) %all-reduce.3.cloned.1.call-update) | async-done | bytes 6291472 | tf_op jit(solution)/shard_map/psum | solution.py:36
  198.9 8.0 %convolution_bitcast_fusion = f32[768,2,1536]{2,0,1:T(8,128)} fusion(bf16[2,512,1536]{2,1,0:T(8,128)(2,1)S(1)} %copy-done, f32[2,2,768,512]{3,2,1,0:T(8,128)} %all-reduce.3.cloned.1.call-done), kind=kOutput, calls=%fused_computation.1 | convolution fusion | flops 2420637696 | bytes 18874368 | tf_op jit(solution)/shard_map/enh,ehd->ned/dot_general | solution.py:39
  206.9 0.7 copy-done.1
  207.6 73.1 %reduce-scatter.2.cloned.1.call-done = f32[48,2,1536]{2,0,1:T(8,128)} async-done(((f32[768,2,1536]{2,0,1:T(8,128)}), f32[48,2,1536]{2,0,1:T(8,128)}) %reduce-scatter.2.cloned.1.call-update) | async-done | bytes 589840 | tf_op jit(solution)/shard_map/reduce_scatter | solution.py:38
  280.7 2.8 convolution_bitcast_fusion.1
  283.5 26.3 %all-reduce.4 = bf16[128,1536]{1,0:T(8,128)(2,1)} all-reduce(f32[128,1536]{1,0:T(8,128)} %convolution_bitcast_fusion.1), channel_id=1, replica_groups=mesh['dp'=16,'expert'=4,'blk'=4] {'expert'}, use_global_device_ids=true, to_apply=%region_7.8 | all-reduce | flops 196608 | bytes 1179648 | tf_op jit(solution)/shard_map/psum | solution.py:45
  (16 shorter events, 0.2 us)
Async XLA Ops:
  6.5 192.3 %copy-start = (bf16[2,512,1536]{2,1,0:T(8,128)(2,1)S(1)}, bf16[2,512,1536]{2,1,0:T(8,128)(2,1)}, u32[]{:S(2)}) copy-start(bf16[2,512,1536]{2,1,0:T(8,128)(2,1)} %param.11) | copy-start | bytes 9437188
  6.5 50.9 %all-gather.2.cloned.1.call-start = ((), (), s32[]{:S(2)}) async-start(), calls=%async_computation.1 | async-start | bytes 5013504 | tf_op jit(solution)/shard_map/all_gather | solution.py:30
  11.7 187.2 %all-reduce.3.cloned.1.call-start = ((), (), s32[]{:S(2)}) async-start(), calls=%async_computation.2 | async-start | bytes 12582912 | tf_op jit(solution)/shard_map/psum | solution.py:36
  57.5 5.6 %copy-start.2 = (bf16[2,768,1536]{2,1,0:T(8,128)(2,1)S(1)}, bf16[2,768,1536]{2,1,0:T(8,128)(2,1)}, u32[]{:S(2)}) copy-start(bf16[2,768,1536]{2,1,0:T(8,128)(2,1)} %all-gather.2.cloned.1.call-done) | copy-start | bytes 14155780
  57.5 5.6 %copy-start.3 = (bf16[2,1536,512]{2,1,0:T(8,128)(2,1)S(1)}, bf16[2,1536,512]{2,1,0:T(8,128)(2,1)}, u32[]{:S(2)}) copy-start(bf16[2,1536,512]{2,1,0:T(8,128)(2,1)} %param.9) | copy-start | bytes 9437188
  69.1 211.6 %reduce-scatter.2.cloned.1.call-start = ((), (), s32[]{:S(2)}) async-start(), calls=%async_computation.3 | async-start | bytes 10027008 | tf_op jit(solution)/shard_map/reduce_scatter | solution.py:38
  206.9 0.7 copy-start.1
Sparse Core Ops, SparseCore 0:
  11.8 45.6 all-gather.1
  69.2 129.6 all-reduce.2
  207.0 73.5 reduce-scatter.1
where the time goes:
time: 316 us
  waiting for transfers between devices  249 us (79%)
  blocking collectives  26.3 us (8%)
  matrix products  20.9 us (7%)
  between operations  13.2 us (4%)
  other arithmetic  4.85 us (2%)
    psum x1, waiting for transfers between devices, local(): summed = lax.psum(partial_value, 'blk')  130 us
    reduce_scatter x1, waiting for transfers between devices, local(): lax.psum_scatter(jnp.einsum('enh,ehd->ned', hidden, down_weight, preferre...  73.1 us
    all_gather x1, waiting for transfers between devices, local(): shard_rows = lax.all_gather(picked, 'dp', axis=1, tiled=True)  45.8 us
    psum x1, blocking collectives, local(): mixed = lax.psum(mixed_part, 'expert')  26.3 us
    dot_general x1, matrix products, local(): jnp.einsum('enh,ehd->ned', hidden, down_weight, preferred_element_type=jn...  8.03 us
  transfers between devices with their start and end apart: 3, of which 3 were waited for; matrix products, arithmetic and copies ran while one was open for 0% of the time, Pallas kernels for 0%

commit v1 on v0

--- a/solution.py
+++ b/solution.py
@@ -27,7 +27,12 @@
     picked = jnp.einsum("tec,tf->ecf", dispatch, tokens, preferred_element_type=jnp.float32).astype(
         jnp.bfloat16
     )
-    shard_rows = lax.all_gather(picked, "dp", axis=1, tiled=True)
+    ring = [picked]
+    for hop in range(15):
+        ring.append(lax.ppermute(ring[-1], "dp", [(dev, (dev + 1) % 16) for dev in range(16)]))
+    shard_rows = jnp.roll(
+        jnp.concatenate(ring[::-1], axis=1), (lax.axis_index("dp") + 1) * ring[0].shape[1], axis=1
+    )
     gate_part = jnp.einsum(
         "enf,efh->enh", shard_rows, gate_weight, preferred_element_type=jnp.float32
     )

time: 316 us -> 410 us (1.30)
  waiting for transfers between devices: 249 us -> 318 us
  local copies, waits for them, and re-layouts: 2.37 us -> 28.7 us
    ppermute x0 -> x15, waiting for transfers between devices: none -> 113 us  [local(): lax.ppermute(ring[-1], 'dp', [(dev, (dev + 1) % 16) for dev in range(16)])]
    all_gather x1 -> x0, waiting for transfers between devices: 45.8 us -> none  [local(): shard_rows = lax.all_gather(picked, 'dp', axis=1, tiled=True)]
    unnamed x9 -> x92, local copies, waits for them, and re-layouts: 1.67 us -> 28 us
  transfers between devices with their start and end apart: 3 -> 17, of which waited for: 3 -> 17; matrix products, arithmetic and copies ran while one was open for 0% -> 0% of each run, Pallas kernels for 0% -> 0%
where the time goes in v1:
time: 410 us; the launch traced here: 409 us
  waiting for transfers between devices  318 us (78%)
  local copies, waits for them, and re-layouts  28.7 us (7%)
  blocking collectives  26.2 us (6%)
  matrix products  17.3 us (4%)
  between operations  13.9 us (3%)
  other arithmetic  4.85 us (1%)
    psum x1, waiting for transfers between devices, local(): summed = lax.psum(partial_value, 'blk')  132 us
    ppermute x15, waiting for transfers between devices, local(): lax.ppermute(ring[-1], 'dp', [(dev, (dev + 1) % 16) for dev in range(16)])  113 us
    reduce_scatter x1, waiting for transfers between devices, local(): lax.psum_scatter(jnp.einsum('enh,ehd->ned', hidden, down_weight, preferre...  73.1 us
    unnamed x92, local copies, waits for them, and re-layouts  28 us
    psum x1, blocking collectives, local(): mixed = lax.psum(mixed_part, 'expert')  26.2 us
  transfers between devices with their start and end apart: 17, of which 17 were waited for; matrix products, arithmetic and copies ran while one was open for 0% of the time, Pallas kernels for 0%

profile of v1, /device:TPU:2, one launch (start us, length us, event | category | flops | bytes accessed | tf_op | source)
XLA Modules:
  0.0 408.9 jit_solution(7172568804399719344)
XLA Ops:
  9.7 1.2 convolution_convert_fusion
  10.9 9.7 %collective-permute-done = bf16[2,48,1536]{2,1,0:T(8,128)(2,1)S(1)} collective-permute-done((bf16[2,48,1536]{2,1,0:T(8,128)(2,1)S(1)}, bf16[2,48,1536]{2,1,0:T(8,128)(2,1)S(1)}, u32[]{:S(2)}, u32[]{:S(2)}) %collective-permute-start) | collective-permute-done | bytes 294944 | tf_op jit(solution)/shard_map/ppermute | solution.py:32
  21.3 7.4 %collective-permute-done.1 = bf16[2,48,1536]{2,1,0:T(8,128)(2,1)S(1)} collective-permute-done((bf16[2,48,1536]{2,1,0:T(8,128)(2,1)S(1)}, bf16[2,48,1536]{2,1,0:T(8,128)(2,1)S(1)}, u32[]{:S(2)}, u32[]{:S(2)}) %collective-permute-start.1) | collective-permute-done | bytes 294944 | tf_op jit(solution)/shard_map/ppermute | solution.py:32
  29.4 7.4 %collective-permute-done.2 = bf16[2,48,1536]{2,1,0:T(8,128)(2,1)S(1)} collective-permute-done((bf16[2,48,1536]{2,1,0:T(8,128)(2,1)S(1)}, bf16[2,48,1536]{2,1,0:T(8,128)(2,1)S(1)}, u32[]{:S(2)}, u32[]{:S(2)}) %collective-permute-start.2) | collective-permute-done | bytes 294944 | tf_op jit(solution)/shard_map/ppermute | solution.py:32
  37.5 7.4 %collective-permute-done.3 = bf16[2,48,1536]{2,1,0:T(8,128)(2,1)S(1)} collective-permute-done((bf16[2,48,1536]{2,1,0:T(8,128)(2,1)S(1)}, bf16[2,48,1536]{2,1,0:T(8,128)(2,1)S(1)}, u32[]{:S(2)}, u32[]{:S(2)}) %collective-permute-start.3) | collective-permute-done | bytes 294944 | tf_op jit(solution)/shard_map/ppermute | solution.py:32
  45.6 7.4 %collective-permute-done.4 = bf16[2,48,1536]{2,1,0:T(8,128)(2,1)S(1)} collective-permute-done((bf16[2,48,1536]{2,1,0:T(8,128)(2,1)S(1)}, bf16[2,48,1536]{2,1,0:T(8,128)(2,1)S(1)}, u32[]{:S(2)}, u32[]{:S(2)}) %collective-permute-start.4) | collective-permute-done | bytes 294944 | tf_op jit(solution)/shard_map/ppermute | solution.py:32
  53.7 7.4 %collective-permute-done.5 = bf16[2,48,1536]{2,1,0:T(8,128)(2,1)S(1)} collective-permute-done((bf16[2,48,1536]{2,1,0:T(8,128)(2,1)S(1)}, bf16[2,48,1536]{2,1,0:T(8,128)(2,1)S(1)}, u32[]{:S(2)}, u32[]{:S(2)}) %collective-permute-start.5) | collective-permute-done | bytes 294944 | tf_op jit(solution)/shard_map/ppermute | solution.py:32
  61.7 7.4 %collective-permute-done.6 = bf16[2,48,1536]{2,1,0:T(8,128)(2,1)S(1)} collective-permute-done((bf16[2,48,1536]{2,1,0:T(8,128)(2,1)S(1)}, bf16[2,48,1536]{2,1,0:T(8,128)(2,1)S(1)}, u32[]{:S(2)}, u32[]{:S(2)}) %collective-permute-start.6) | collective-permute-done | bytes 294944 | tf_op jit(solution)/shard_map/ppermute | solution.py:32
  69.8 7.4 %collective-permute-done.7 = bf16[2,48,1536]{2,1,0:T(8,128)(2,1)S(1)} collective-permute-done((bf16[2,48,1536]{2,1,0:T(8,128)(2,1)S(1)}, bf16[2,48,1536]{2,1,0:T(8,128)(2,1)S(1)}, u32[]{:S(2)}, u32[]{:S(2)}) %collective-permute-start.7) | collective-permute-done | bytes 294944 | tf_op jit(solution)/shard_map/ppermute | solution.py:32
  77.9 7.4 %collective-permute-done.8 = bf16[2,48,1536]{2,1,0:T(8,128)(2,1)S(1)} collective-permute-done((bf16[2,48,1536]{2,1,0:T(8,128)(2,1)S(1)}, bf16[2,48,1536]{2,1,0:T(8,128)(2,1)S(1)}, u32[]{:S(2)}, u32[]{:S(2)}) %collective-permute-start.8) | collective-permute-done | bytes 294944 | tf_op jit(solution)/shard_map/ppermute | solution.py:32
  86.0 7.4 %collective-permute-done.9 = bf16[2,48,1536]{2,1,0:T(8,128)(2,1)S(1)} collective-permute-done((bf16[2,48,1536]{2,1,0:T(8,128)(2,1)S(1)}, bf16[2,48,1536]{2,1,0:T(8,128)(2,1)S(1)}, u32[]{:S(2)}, u32[]{:S(2)}) %collective-permute-start.9) | collective-permute-done | bytes 294944 | tf_op jit(solution)/shard_map/ppermute | solution.py:32
  94.1 7.4 %collective-permute-done.10 = bf16[2,48,1536]{2,1,0:T(8,128)(2,1)S(1)} collective-permute-done((bf16[2,48,1536]{2,1,0:T(8,128)(2,1)S(1)}, bf16[2,48,1536]{2,1,0:T(8,128)(2,1)S(1)}, u32[]{:S(2)}, u32[]{:S(2)}) %collective-permute-start.10) | collective-permute-done | bytes 294944 | tf_op jit(solution)/shard_map/ppermute | solution.py:32
  102.1 7.4 %collective-permute-done.11 = bf16[2,48,1536]{2,1,0:T(8,128)(2,1)S(1)} collective-permute-done((bf16[2,48,1536]{2,1,0:T(8,128)(2,1)S(1)}, bf16[2,48,1536]{2,1,0:T(8,128)(2,1)S(1)}, u32[]{:S(2)}, u32[]{:S(2)}) %collective-permute-start.11) | collective-permute-done | bytes 294944 | tf_op jit(solution)/shard_map/ppermute | solution.py:32
  110.2 7.4 %collective-permute-done.12 = bf16[2,48,1536]{2,1,0:T(8,128)(2,1)S(1)} collective-permute-done((bf16[2,48,1536]{2,1,0:T(8,128)(2,1)S(1)}, bf16[2,48,1536]{2,1,0:T(8,128)(2,1)S(1)}, u32[]{:S(2)}, u32[]{:S(2)}) %collective-permute-start.12) | collective-permute-done | bytes 294944 | tf_op jit(solution)/shard_map/ppermute | solution.py:32
  118.3 7.5 %collective-permute-done.13 = bf16[2,48,1536]{2,1,0:T(8,128)(2,1)} collective-permute-done((bf16[2,48,1536]{2,1,0:T(8,128)(2,1)S(1)}, bf16[2,48,1536]{2,1,0:T(8,128)(2,1)}, u32[]{:S(2)}, u32[]{:S(2)}) %collective-permute-start.13) | collective-permute-done | bytes 294944 | tf_op jit(solution)/shard_map/ppermute | solution.py:32
  125.9 7.5 %collective-permute-done.14 = bf16[2,48,1536]{2,1,0:T(8,128)(2,1)} collective-permute-done((bf16[2,48,1536]{2,1,0:T(8,128)(2,1)}, bf16[2,48,1536]{2,1,0:T(8,128)(2,1)}, u32[]{:S(2)}, u32[]{:S(2)}) %collective-permute-start.14) | collective-permute-done | bytes 294944 | tf_op jit(solution)/shard_map/ppermute | solution.py:32
  150.8 2.6 fusion.6
  153.4 2.6 fusion.9
  156.0 3.4 pad_maximum_fusion
  159.4 131.7 %all-reduce.3.cloned.1.call-done = f32[2,2,768,512]{3,2,1,0:T(8,128)} async-done(((f32[2,2,768,512]{3,2,1,0:T(8,128)}), f32[2,2,768,512]{3,2,1,0:T(8,128)}) %all-reduce.3.cloned.1.call-update) | async-done | bytes 6291472 | tf_op jit(solution)/shard_map/psum | solution.py:41
  291.1 8.1 %convolution_bitcast_fusion = f32[768,2,1536]{2,0,1:T(8,128)} fusion(bf16[2,512,1536]{2,1,0:T(8,128)(2,1)S(1)} %copy-done, f32[2,2,768,512]{3,2,1,0:T(8,128)} %all-reduce.3.cloned.1.call-done), kind=kOutput, calls=%fused_computation.1 | convolution fusion | flops 2420637696 | bytes 18874368 | tf_op jit(solution)/shard_map/enh,ehd->ned/dot_general | solution.py:44
  299.9 73.1 %reduce-scatter.2.cloned.1.call-done = f32[48,2,1536]{2,0,1:T(8,128)} async-done(((f32[768,2,1536]{2,0,1:T(8,128)}), f32[48,2,1536]{2,0,1:T(8,128)}) %reduce-scatter.2.cloned.1.call-update) | async-done | bytes 589840 | tf_op jit(solution)/shard_map/reduce_scatter | solution.py:43
  373.0 2.8 convolution_bitcast_fusion.1
  375.8 26.2 %all-reduce.4 = bf16[128,1536]{1,0:T(8,128)(2,1)} all-reduce(f32[128,1536]{1,0:T(8,128)} %convolution_bitcast_fusion.1), channel_id=1, replica_groups=mesh['dp'=16,'expert'=4,'blk'=4] {'expert'}, use_global_device_ids=true, to_apply=%region_7.8 | all-reduce | flops 196608 | bytes 1179648 | tf_op jit(solution)/shard_map/psum | solution.py:50
  (127 shorter events, 30.3 us)
Async XLA Ops:
  6.5 284.6 %copy-start = (bf16[2,512,1536]{2,1,0:T(8,128)(2,1)S(1)}, bf16[2,512,1536]{2,1,0:T(8,128)(2,1)}, u32[]{:S(2)}) copy-start(bf16[2,512,1536]{2,1,0:T(8,128)(2,1)} %param.11) | copy-start | bytes 9437188
  6.5 284.6 %all-reduce.3.cloned.1.call-start = ((), (), s32[]{:S(2)}) async-start(), calls=%async_computation.1 | async-start | bytes 12582912 | tf_op jit(solution)/shard_map/psum | solution.py:41
  10.9 9.7 %collective-permute-start = (bf16[2,48,1536]{2,1,0:T(8,128)(2,1)S(1)}, bf16[2,48,1536]{2,1,0:T(8,128)(2,1)S(1)}, u32[]{:S(2)}, u32[]{:S(2)}) collective-permute-start(bf16[2,48,1536]{2,1,0:T(8,128)(2,1)S(1)} %convolution_convert_fusion), channel_id=1, source_target_pairs={{0,16},{16,32},{32,48},{48,64},{64,80},{80,96},{96,112},{112,128},... | collective-permute-start | bytes 884744 | tf_op jit(solution)/shard_map/ppermute | solution.py:32
  21.3 7.4 %collective-permute-start.1 = (bf16[2,48,1536]{2,1,0:T(8,128)(2,1)S(1)}, bf16[2,48,1536]{2,1,0:T(8,128)(2,1)S(1)}, u32[]{:S(2)}, u32[]{:S(2)}) collective-permute-start(bf16[2,48,1536]{2,1,0:T(8,128)(2,1)S(1)} %collective-permute-done), channel_id=1, source_target_pairs={{0,16},{16,32},{32,48},{48,64},{64,80},{80,96},{96,112},{112,128},... | collective-permute-start | bytes 884744 | tf_op jit(solution)/shard_map/ppermute | solution.py:32
  29.4 7.4 %collective-permute-start.2 = (bf16[2,48,1536]{2,1,0:T(8,128)(2,1)S(1)}, bf16[2,48,1536]{2,1,0:T(8,128)(2,1)S(1)}, u32[]{:S(2)}, u32[]{:S(2)}) collective-permute-start(bf16[2,48,1536]{2,1,0:T(8,128)(2,1)S(1)} %collective-permute-done.1), channel_id=1, source_target_pairs={{0,16},{16,32},{32,48},{48,64},{64,80},{80,96},{96,112},{112,128},... | collective-permute-start | bytes 884744 | tf_op jit(solution)/shard_map/ppermute | solution.py:32
  37.5 7.4 %collective-permute-start.3 = (bf16[2,48,1536]{2,1,0:T(8,128)(2,1)S(1)}, bf16[2,48,1536]{2,1,0:T(8,128)(2,1)S(1)}, u32[]{:S(2)}, u32[]{:S(2)}) collective-permute-start(bf16[2,48,1536]{2,1,0:T(8,128)(2,1)S(1)} %collective-permute-done.2), channel_id=1, source_target_pairs={{0,16},{16,32},{32,48},{48,64},{64,80},{80,96},{96,112},{112,128},... | collective-permute-start | bytes 884744 | tf_op jit(solution)/shard_map/ppermute | solution.py:32
  45.6 7.4 %collective-permute-start.4 = (bf16[2,48,1536]{2,1,0:T(8,128)(2,1)S(1)}, bf16[2,48,1536]{2,1,0:T(8,128)(2,1)S(1)}, u32[]{:S(2)}, u32[]{:S(2)}) collective-permute-start(bf16[2,48,1536]{2,1,0:T(8,128)(2,1)S(1)} %collective-permute-done.3), channel_id=1, source_target_pairs={{0,16},{16,32},{32,48},{48,64},{64,80},{80,96},{96,112},{112,128},... | collective-permute-start | bytes 884744 | tf_op jit(solution)/shard_map/ppermute | solution.py:32
  53.7 7.4 %collective-permute-start.5 = (bf16[2,48,1536]{2,1,0:T(8,128)(2,1)S(1)}, bf16[2,48,1536]{2,1,0:T(8,128)(2,1)S(1)}, u32[]{:S(2)}, u32[]{:S(2)}) collective-permute-start(bf16[2,48,1536]{2,1,0:T(8,128)(2,1)S(1)} %collective-permute-done.4), channel_id=1, source_target_pairs={{0,16},{16,32},{32,48},{48,64},{64,80},{80,96},{96,112},{112,128},... | collective-permute-start | bytes 884744 | tf_op jit(solution)/shard_map/ppermute | solution.py:32
  61.7 7.4 %collective-permute-start.6 = (bf16[2,48,1536]{2,1,0:T(8,128)(2,1)S(1)}, bf16[2,48,1536]{2,1,0:T(8,128)(2,1)S(1)}, u32[]{:S(2)}, u32[]{:S(2)}) collective-permute-start(bf16[2,48,1536]{2,1,0:T(8,128)(2,1)S(1)} %collective-permute-done.5), channel_id=1, source_target_pairs={{0,16},{16,32},{32,48},{48,64},{64,80},{80,96},{96,112},{112,128},... | collective-permute-start | bytes 884744 | tf_op jit(solution)/shard_map/ppermute | solution.py:32
  69.8 7.4 %collective-permute-start.7 = (bf16[2,48,1536]{2,1,0:T(8,128)(2,1)S(1)}, bf16[2,48,1536]{2,1,0:T(8,128)(2,1)S(1)}, u32[]{:S(2)}, u32[]{:S(2)}) collective-permute-start(bf16[2,48,1536]{2,1,0:T(8,128)(2,1)S(1)} %collective-permute-done.6), channel_id=1, source_target_pairs={{0,16},{16,32},{32,48},{48,64},{64,80},{80,96},{96,112},{112,128},... | collective-permute-start | bytes 884744 | tf_op jit(solution)/shard_map/ppermute | solution.py:32
  77.9 7.4 %collective-permute-start.8 = (bf16[2,48,1536]{2,1,0:T(8,128)(2,1)S(1)}, bf16[2,48,1536]{2,1,0:T(8,128)(2,1)S(1)}, u32[]{:S(2)}, u32[]{:S(2)}) collective-permute-start(bf16[2,48,1536]{2,1,0:T(8,128)(2,1)S(1)} %collective-permute-done.7), channel_id=1, source_target_pairs={{0,16},{16,32},{32,48},{48,64},{64,80},{80,96},{96,112},{112,128},... | collective-permute-start | bytes 884744 | tf_op jit(solution)/shard_map/ppermute | solution.py:32
  86.0 7.4 %collective-permute-start.9 = (bf16[2,48,1536]{2,1,0:T(8,128)(2,1)S(1)}, bf16[2,48,1536]{2,1,0:T(8,128)(2,1)S(1)}, u32[]{:S(2)}, u32[]{:S(2)}) collective-permute-start(bf16[2,48,1536]{2,1,0:T(8,128)(2,1)S(1)} %collective-permute-done.8), channel_id=1, source_target_pairs={{0,16},{16,32},{32,48},{48,64},{64,80},{80,96},{96,112},{112,128},... | collective-permute-start | bytes 884744 | tf_op jit(solution)/shard_map/ppermute | solution.py:32
  94.1 7.4 %collective-permute-start.10 = (bf16[2,48,1536]{2,1,0:T(8,128)(2,1)S(1)}, bf16[2,48,1536]{2,1,0:T(8,128)(2,1)S(1)}, u32[]{:S(2)}, u32[]{:S(2)}) collective-permute-start(bf16[2,48,1536]{2,1,0:T(8,128)(2,1)S(1)} %collective-permute-done.9), channel_id=1, source_target_pairs={{0,16},{16,32},{32,48},{48,64},{64,80},{80,96},{96,112},{112,128},... | collective-permute-start | bytes 884744 | tf_op jit(solution)/shard_map/ppermute | solution.py:32
  102.1 7.4 %collective-permute-start.11 = (bf16[2,48,1536]{2,1,0:T(8,128)(2,1)S(1)}, bf16[2,48,1536]{2,1,0:T(8,128)(2,1)S(1)}, u32[]{:S(2)}, u32[]{:S(2)}) collective-permute-start(bf16[2,48,1536]{2,1,0:T(8,128)(2,1)S(1)} %collective-permute-done.10), channel_id=1, source_target_pairs={{0,16},{16,32},{32,48},{48,64},{64,80},{80,96},{96,112},{112,128},... | collective-permute-start | bytes 884744 | tf_op jit(solution)/shard_map/ppermute | solution.py:32
  110.2 7.4 %collective-permute-start.12 = (bf16[2,48,1536]{2,1,0:T(8,128)(2,1)S(1)}, bf16[2,48,1536]{2,1,0:T(8,128)(2,1)S(1)}, u32[]{:S(2)}, u32[]{:S(2)}) collective-permute-start(bf16[2,48,1536]{2,1,0:T(8,128)(2,1)S(1)} %collective-permute-done.11), channel_id=1, source_target_pairs={{0,16},{16,32},{32,48},{48,64},{64,80},{80,96},{96,112},{112,128},... | collective-permute-start | bytes 884744 | tf_op jit(solution)/shard_map/ppermute | solution.py:32
  118.3 7.5 %collective-permute-start.13 = (bf16[2,48,1536]{2,1,0:T(8,128)(2,1)S(1)}, bf16[2,48,1536]{2,1,0:T(8,128)(2,1)}, u32[]{:S(2)}, u32[]{:S(2)}) collective-permute-start(bf16[2,48,1536]{2,1,0:T(8,128)(2,1)S(1)} %collective-permute-done.12), channel_id=1, source_target_pairs={{0,16},{16,32},{32,48},{48,64},{64,80},{80,96},{96,112},{112,128},... | collective-permute-start | bytes 884744 | tf_op jit(solution)/shard_map/ppermute | solution.py:32
  125.7 7.7 %collective-permute-start.14 = (bf16[2,48,1536]{2,1,0:T(8,128)(2,1)}, bf16[2,48,1536]{2,1,0:T(8,128)(2,1)}, u32[]{:S(2)}, u32[]{:S(2)}) collective-permute-start(bf16[2,48,1536]{2,1,0:T(8,128)(2,1)} %collective-permute-done.13), channel_id=1, source_target_pairs={{0,16},{16,32},{32,48},{48,64},{64,80},{80,96},{96,112},{112,128},... | collective-permute-start | bytes 884744 | tf_op jit(solution)/shard_map/ppermute | solution.py:32
  125.8 24.7 %copy-start.10 = (bf16[2,48,1536]{2,1,0:T(8,128)(2,1)S(1)}, bf16[2,48,1536]{2,1,0:T(8,128)(2,1)}, u32[]{:S(2)}) copy-start(bf16[2,48,1536]{2,1,0:T(8,128)(2,1)} %copy-done.9) | copy-start | bytes 884740
  125.8 24.7 %copy-start.8 = (bf16[2,48,1536]{2,1,0:T(8,128)(2,1)S(1)}, bf16[2,48,1536]{2,1,0:T(8,128)(2,1)}, u32[]{:S(2)}) copy-start(bf16[2,48,1536]{2,1,0:T(8,128)(2,1)} %copy-done.7) | copy-start | bytes 884740
  125.8 24.8 %copy-start.6 = (bf16[2,48,1536]{2,1,0:T(8,128)(2,1)S(1)}, bf16[2,48,1536]{2,1,0:T(8,128)(2,1)}, u32[]{:S(2)}) copy-start(bf16[2,48,1536]{2,1,0:T(8,128)(2,1)} %copy-done.5) | copy-start | bytes 884740
  125.8 24.8 %copy-start.4 = (bf16[2,48,1536]{2,1,0:T(8,128)(2,1)S(1)}, bf16[2,48,1536]{2,1,0:T(8,128)(2,1)}, u32[]{:S(2)}) copy-start(bf16[2,48,1536]{2,1,0:T(8,128)(2,1)} %copy-done.3) | copy-start | bytes 884740
  125.8 24.8 %copy-start.2 = (bf16[2,48,1536]{2,1,0:T(8,128)(2,1)S(1)}, bf16[2,48,1536]{2,1,0:T(8,128)(2,1)}, u32[]{:S(2)}) copy-start(bf16[2,48,1536]{2,1,0:T(8,128)(2,1)} %copy-done.1) | copy-start | bytes 884740
  125.9 24.9 %copy-start.28 = (bf16[2,1536,512]{2,1,0:T(8,128)(2,1)S(1)}, bf16[2,1536,512]{2,1,0:T(8,128)(2,1)}, u32[]{:S(2)}) copy-start(bf16[2,1536,512]{2,1,0:T(8,128)(2,1)} %param.9) | copy-start | bytes 9437188
  159.4 213.6 %reduce-scatter.2.cloned.1.call-start = ((), (), s32[]{:S(2)}) async-start(), calls=%async_computation.2 | async-start | bytes 10027008 | tf_op jit(solution)/shard_map/reduce_scatter | solution.py:43
  (23 other events, 209.4 us)
Sparse Core Ops, SparseCore 0:
  159.5 131.5 all-reduce.2
  299.4 73.6 reduce-scatter.1
